TPU v7x, 32 devices: a whole 2x2x4 slice. The times are simulated.
32 devices in a mesh: sec: 8 (over y, x, core), tile: 4 (over z).
Axes of the slice: x: 2, y: 2, z: 4, core: 2. Of those that a mesh axis runs over, the one named last changes fastest.
Arguments:
- displacement: float32 [2, 16, 32, 2048], P(None, 'sec', 'tile'), may hold values from -6 to 6
- velocity: float32 [2, 16, 32, 2048], P(None, 'sec', 'tile'), may hold values from -10 to 10
- frac: bfloat16 [2, 4, 16, 32, 2048], P(None, None, 'sec', 'tile'), may hold values from 0 to 1
- offsets: int32 [4, 16, 4, 2], P(None, 'sec', 'tile'), may hold values from -2 to 2
- fixed: int32 [16, 32, 2048], P('sec', 'tile'), may hold values 0 or 1
- trans: float32 [16, 2], P('sec'), may hold values from -0.3 to 0.3
Outputs:
- new_displacement: float32 [2, 16, 32, 2048], P(None, 'sec', 'tile')
- new_velocity: float32 [2, 16, 32, 2048], P(None, 'sec', 'tile')
All inputs are finite; a program needn't handle non-finite values. No bound on the sum of `fixed` on one device may be relied on, other than what follows from the above.
Results may differ from a plain program's by a relative error of at most 0.0003.
Values sent between devices are 32-bit elements; how exact they have to be, the bound alone decides.
A program may use at most 64 MiB of HBM per device.

v0:
```python
import jax
import jax.numpy as jnp
from jax import lax
from jax.sharding import PartitionSpec as P

ITERS = 3


in_stiff = 1.0
anchor_stiff = 0.25
cross_stiff = (0.25, 0.5, 0.5, 0.25)
reaches = (-2, -1, 1, 2)


def carried_in(part, axis, combine, identity):
    place = lax.axis_index(axis)
    gathered = lax.all_gather(part, axis)
    state = jnp.zeros_like(part) + jnp.asarray(identity, part.dtype)

    def one(turn, state):
        return combine(state, lax.dynamic_index_in_dim(gathered, turn, 0, False))

    return lax.fori_loop(0, place, one, state)


def padded(cells, sides, width):
    for axis, dim in sides:
        count = lax.axis_size(axis)
        ends = count - 1
        head = lax.slice_in_dim(cells, 0, width, axis=dim)
        tail = lax.slice_in_dim(cells, cells.shape[dim] - width, cells.shape[dim], axis=dim)
        cells = jnp.concatenate(
            [
                lax.ppermute(tail, axis, [(i, (i + 1) % count) for i in range(ends)]),
                cells,
                lax.ppermute(head, axis, [((i + 1) % count, i) for i in range(ends)]),
            ],
            axis=dim,
        )
    return cells


def spring_force(ext, frac, offsets, fixed, anchor, sec_first, row_first, sections, rows):
    count = fixed.shape[0]
    height = fixed.shape[1]
    width = fixed.shape[2]
    centre = ext[:, 2 : count + 2, 3 : height + 3, :]
    grow = row_first + jnp.arange(height, dtype=jnp.int32)
    gcol = jnp.arange(width, dtype=jnp.int32)
    gsec = sec_first + jnp.arange(count, dtype=jnp.int32)
    above = ext[:, 2 : count + 2, 2 : height + 2, :]
    below = ext[:, 2 : count + 2, 4 : height + 4, :]
    left = jnp.roll(centre, 1, axis=3)
    right = jnp.roll(centre, -1, axis=3)
    force = jnp.where((grow > 0)[:, None], above - centre, 0.0)
    force = force + jnp.where((grow < rows - 1)[:, None], below - centre, 0.0)
    force = force + jnp.where((gcol > 0)[None, :], left - centre, 0.0)
    force = force + jnp.where((gcol < width - 1)[None, :], right - centre, 0.0)
    force = in_stiff * force + anchor_stiff * (jnp.transpose(anchor)[:, :, None, None] - centre)
    for index in range(4):
        reach = reaches[index]
        stiff = cross_stiff[index]
        source = ext[:, 2 + reach : 2 + reach + count]

        def pull(block, frow, fcol, shift, own, section):
            frow = frow.astype(jnp.float32)
            fcol = fcol.astype(jnp.float32)
            part_rows = lax.dynamic_slice_in_dim(block, 3 + shift[0], height + 1, 1)
            first = jnp.roll(part_rows, -shift[1], axis=2)
            second = jnp.roll(part_rows, -shift[1] - 1, axis=2)
            match = (1.0 - frow) * ((1.0 - fcol) * first[:, :height] + fcol * second[:, :height])
            match = match + frow * ((1.0 - fcol) * first[:, 1:] + fcol * second[:, 1:])
            flow = jnp.stack(
                [shift[0].astype(jnp.float32) + frow, shift[1].astype(jnp.float32) + fcol]
            )
            gap = match + flow - own
            row_ok = (grow + shift[0] >= 0) & (grow + shift[0] + 1 <= rows - 1)
            col_ok = (gcol + shift[1] >= 0) & (gcol + shift[1] + 1 <= width - 1)
            sec_ok = (section + reach >= 0) & (section + reach < sections)
            valid = row_ok[:, None] & col_ok[None, :] & sec_ok
            return jnp.where(valid, stiff * gap, 0.0)

        force = force + jax.vmap(pull, in_axes=(1, 0, 0, 0, 1, 0), out_axes=1)(
            source, frac[0, index], frac[1, index], offsets[index], centre, gsec
        )
    return force * (1 - fixed).astype(jnp.float32)[None]


def add_pair(earlier, later):
    return earlier + later


def shards(displacement, velocity, frac, offsets, fixed, trans):
    count = displacement.shape[1]
    height = displacement.shape[2]
    sections = count * lax.axis_size("sec")
    rows = height * lax.axis_size("tile")
    sec_first = lax.axis_index("sec") * count
    row_first = lax.axis_index("tile") * height
    local = jnp.cumsum(trans, 0)
    before = carried_in(local[-1], "sec", add_pair, jnp.zeros((2,), jnp.float32))
    anchor = local + before[None, :]
    tile_shift = offsets[:, :, 0, :]
    keep = (1 - fixed).astype(jnp.float32)
    moving = velocity * keep[None]
    shifted = displacement
    for step in range(ITERS):
        alpha = 0.1 * 0.99**step
        delta = 0.25 * 1.1**step
        taller = padded(shifted, (("tile", 2),), 3)
        ext = padded(taller, (("sec", 1),), 2)
        force = spring_force(
            ext, frac, tile_shift, fixed, anchor, sec_first, row_first, sections, rows
        )
        ff, vv = lax.psum((jnp.sum(force * force), jnp.sum(moving * moving)), ("sec", "tile"))
        ratio = jnp.sqrt(vv / (ff + 1e-06))
        moving = (1.0 - alpha) * moving + alpha * ratio * force
        moving = moving + delta * force
        shifted = shifted + delta * moving
    return (shifted, moving)


def solution(mesh):
    placed = (
        P(None, "sec", "tile", None),
        P(None, "sec", "tile", None),
        P(None, None, "sec", "tile", None),
        P(None, "sec", "tile", None),
        P("sec", "tile", None),
        P("sec", None),
    )
    return jax.shard_map(
        shards,
        mesh=mesh,
        in_specs=placed,
        out_specs=(P(None, "sec", "tile", None), P(None, "sec", "tile", None)),
        check_vma=False,
    )
```

profile of v0, /device:TPU:0, one launch (start us, length us, event | category | flops | bytes accessed | tf_op | source)
XLA Modules:
  0.0 445.5 jit_solution(2538900548368978884)
XLA Ops:
  1.8 4.9 %collective-permute-start = (f32[2,2,3,2048]{3,2,1,0:T(4,128)S(1)}, f32[2,2,3,2048]{3,2,1,0:T(4,128)S(1)}, u32[]{:S(2)}, u32[]{:S(2)}) collective-permute-start(f32[2,2,3,2048]{3,2,1,0:T(4,128)S(1)} %get-tuple-element.932), channel_id=1, source_target_pairs={{0,1},{1,2},{2,3},{4,5},{5,6},{6,7},{8,9},{9,10},{10,11},{12,13},{... | collective-permute-start | bytes 294920 | tf_op jit(solution)/shard_map/ppermute | solution.py:34
  19.6 8.7 %all-gather = f32[8,1,2]{2,1,0:T(1,128)S(1)} all-gather(f32[1,1,2]{2,1,0:T(1,128)S(1)} %slice_bitcast_fusion), channel_id=1, replica_groups=mesh['sec'=8,'tile'=4] {'sec'}, dimensions={0}, use_global_device_ids=true | all-gather | bytes 72 | tf_op jit(solution)/shard_map/all_gather | solution.py:17
  44.1 6.8 %while.61 = (s32[]{:T(128)}, f32[2,2,9,4096]{3,2,1,0:T(8,128)S(1)}, s32[2,4]{1,0:T(2,128)}, f32[2,2,9,2048]{3,2,0,1:T(8,128)}, s32[]{:T(128)}) while((s32[]{:T(128)}, f32[2,2,9,4096]{3,2,1,0:T(8,128)S(1)}, s32[2,4]{1,0:T(2,128)}, f32[2,2,9,2048]{3,2,0,1:T(8,128)}, s32[]{:T(128)}) %tuple.556), condition=%wide.while_cond.clone.1, body=%wide.while_body.clone.1.sunk | while | flops 2 | bytes 411405 | solution.py:69
  51.7 6.9 %while.62 = (s32[]{:T(128)}, f32[2,2,9,4096]{3,2,1,0:T(8,128)S(1)}, s32[2,4]{1,0:T(2,128)}, f32[2,2,9,2048]{3,2,0,1:T(8,128)}, s32[]{:T(128)}) while((s32[]{:T(128)}, f32[2,2,9,4096]{3,2,1,0:T(8,128)S(1)}, s32[2,4]{1,0:T(2,128)}, f32[2,2,9,2048]{3,2,0,1:T(8,128)}, s32[]{:T(128)}) %tuple.620), condition=%wide.while_cond.clone.2, body=%wide.while_body.clone.2.sunk | while | flops 2 | bytes 411405 | solution.py:70
  61.6 5.4 %while.63 = (s32[]{:T(128)}, f32[2,2,9,4096]{3,2,1,0:T(8,128)S(1)}, s32[2,4]{1,0:T(2,128)S(1)}, f32[2,2,9,2048]{3,2,0,1:T(8,128)}, s32[]{:T(128)}) while((s32[]{:T(128)}, f32[2,2,9,4096]{3,2,1,0:T(8,128)S(1)}, s32[2,4]{1,0:T(2,128)S(1)}, f32[2,2,9,2048]{3,2,0,1:T(8,128)}, s32[]{:T(128)}) %tuple.639), condition=%wide.while_cond.clone.3, body=%wide.while_body.clone.3.sunk | while | flops 2 | bytes 411249 | solution.py:69
  67.8 5.4 %while.64 = (s32[]{:T(128)}, f32[2,2,9,4096]{3,2,1,0:T(8,128)S(1)}, s32[2,4]{1,0:T(2,128)S(1)}, f32[2,2,9,2048]{3,2,0,1:T(8,128)}, s32[]{:T(128)}) while((s32[]{:T(128)}, f32[2,2,9,4096]{3,2,1,0:T(8,128)S(1)}, s32[2,4]{1,0:T(2,128)S(1)}, f32[2,2,9,2048]{3,2,0,1:T(8,128)}, s32[]{:T(128)}) %tuple.637), condition=%wide.while_cond.clone.4, body=%wide.while_body.clone.4.sunk | while | flops 2 | bytes 411249 | solution.py:70
  81.0 5.2 %while.60 = (s32[]{:T(128)}, f32[2,2,9,4096]{3,2,1,0:T(8,128)S(1)}, s32[2,4]{1,0:T(2,128)S(1)}, f32[2,2,9,2048]{3,2,0,1:T(8,128)}, s32[]{:T(128)}) while((s32[]{:T(128)}, f32[2,2,9,4096]{3,2,1,0:T(8,128)S(1)}, s32[2,4]{1,0:T(2,128)S(1)}, f32[2,2,9,2048]{3,2,0,1:T(8,128)}, s32[]{:T(128)}) %tuple.633), condition=%wide.while_cond.clone, body=%wide.while_body.clone.sunk | while | flops 2 | bytes 411249 | solution.py:70
  93.8 5.7 %while.66 = (s32[]{:T(128)}, f32[2,2,9,4096]{3,2,1,0:T(8,128)S(1)}, s32[2,4]{1,0:T(2,128)S(1)}, f32[2,2,9,2048]{3,2,0,1:T(8,128)}, s32[]{:T(128)}) while((s32[]{:T(128)}, f32[2,2,9,4096]{3,2,1,0:T(8,128)S(1)}, s32[2,4]{1,0:T(2,128)S(1)}, f32[2,2,9,2048]{3,2,0,1:T(8,128)}, s32[]{:T(128)}) %tuple.629), condition=%wide.while_cond.clone.6, body=%wide.while_body.clone.6.sunk | while | flops 2 | bytes 411249 | solution.py:70
  100.2 5.1 %multiply_reduce_fusion.4 = (f32[]{:T(128)}, f32[2,2,8,2048]{3,2,1,0:T(8,128)S(1)}) fusion(f32[2,8,2048]{2,1,0:T(8,128)S(1)} %subtract_convert_fusion, f32[1,2,8,2048]{3,2,1,0:T(8,128)} %get-tuple-element.912, f32[1,2,8,2048]{3,2,1,0:T(8,128)} %get-tuple-element.911, f32[2,2,9,2048]{3,2,0,1:T(8,128)} %get-tuple-element.180, ...), kind=kLoop, calls=%fused_computation.203 | loop fusion | flops 5308415 | bytes 8851492 | tf_op jit(solution)/shard_map/reduce_sum | solution.py:115
  105.3 48.3 %all-reduce.3 = (f32[]{:T(128)}, f32[]{:T(128)}) all-reduce(f32[]{:T(128)} %multiply_reduce_fusion.5, f32[]{:T(128)} %get-tuple-element.835), channel_id=1, replica_groups=mesh['sec'=8,'tile'=4] {'sec','tile'}, use_global_device_ids=true, to_apply=%region_1.2 | all-reduce | flops 2 | bytes 16 | tf_op jit(solution)/shard_map/psum | solution.py:115
  161.7 4.4 collective-permute-done.5
  177.8 5.5 %while.69 = (s32[]{:T(128)}, f32[2,2,9,4096]{3,2,1,0:T(8,128)S(1)}, s32[2,4]{1,0:T(2,128)S(1)}, f32[2,2,9,2048]{3,2,0,1:T(8,128)}, s32[]{:T(128)}) while((s32[]{:T(128)}, f32[2,2,9,4096]{3,2,1,0:T(8,128)S(1)}, s32[2,4]{1,0:T(2,128)S(1)}, f32[2,2,9,2048]{3,2,0,1:T(8,128)}, s32[]{:T(128)}) %tuple.643), condition=%wide.while_cond.clone.9, body=%wide.while_body.clone.9.sunk | while | flops 2 | bytes 411249 | solution.py:69
  184.2 5.5 %while.70 = (s32[]{:T(128)}, f32[2,2,9,4096]{3,2,1,0:T(8,128)S(1)}, s32[2,4]{1,0:T(2,128)S(1)}, f32[2,2,9,2048]{3,2,0,1:T(8,128)}, s32[]{:T(128)}) while((s32[]{:T(128)}, f32[2,2,9,4096]{3,2,1,0:T(8,128)S(1)}, s32[2,4]{1,0:T(2,128)S(1)}, f32[2,2,9,2048]{3,2,0,1:T(8,128)}, s32[]{:T(128)}) %tuple.641), condition=%wide.while_cond.clone.10, body=%wide.while_body.clone.10.sunk | while | flops 2 | bytes 411249 | solution.py:70
  193.5 6.8 %while.71 = (s32[]{:T(128)}, f32[2,2,9,4096]{3,2,1,0:T(8,128)S(1)}, s32[2,4]{1,0:T(2,128)}, f32[2,2,9,2048]{3,2,0,1:T(8,128)}, s32[]{:T(128)}) while((s32[]{:T(128)}, f32[2,2,9,4096]{3,2,1,0:T(8,128)S(1)}, s32[2,4]{1,0:T(2,128)}, f32[2,2,9,2048]{3,2,0,1:T(8,128)}, s32[]{:T(128)}) %tuple.577), condition=%wide.while_cond.clone.11, body=%wide.while_body.clone.11.sunk | while | flops 2 | bytes 411249 | solution.py:69
  201.1 6.9 %while.72 = (s32[]{:T(128)}, f32[2,2,9,4096]{3,2,1,0:T(8,128)S(1)}, s32[2,4]{1,0:T(2,128)}, f32[2,2,9,2048]{3,2,0,1:T(8,128)}, s32[]{:T(128)}) while((s32[]{:T(128)}, f32[2,2,9,4096]{3,2,1,0:T(8,128)S(1)}, s32[2,4]{1,0:T(2,128)}, f32[2,2,9,2048]{3,2,0,1:T(8,128)}, s32[]{:T(128)}) %tuple.625), condition=%wide.while_cond.clone.12, body=%wide.while_body.clone.12.sunk | while | flops 2 | bytes 411249 | solution.py:70
  211.8 6.6 %while.67 = (s32[]{:T(128)}, f32[2,2,9,4096]{3,2,1,0:T(8,128)S(1)}, s32[2,4]{1,0:T(2,128)}, f32[2,2,9,2048]{3,2,0,1:T(8,128)}, s32[]{:T(128)}) while((s32[]{:T(128)}, f32[2,2,9,4096]{3,2,1,0:T(8,128)S(1)}, s32[2,4]{1,0:T(2,128)}, f32[2,2,9,2048]{3,2,0,1:T(8,128)}, s32[]{:T(128)}) %tuple.589), condition=%wide.while_cond.clone.7, body=%wide.while_body.clone.7.sunk | while | flops 2 | bytes 411249 | solution.py:69
  219.3 6.7 %while.68 = (s32[]{:T(128)}, f32[2,2,9,4096]{3,2,1,0:T(8,128)S(1)}, s32[2,4]{1,0:T(2,128)}, f32[2,2,9,2048]{3,2,0,1:T(8,128)}, s32[]{:T(128)}) while((s32[]{:T(128)}, f32[2,2,9,4096]{3,2,1,0:T(8,128)S(1)}, s32[2,4]{1,0:T(2,128)}, f32[2,2,9,2048]{3,2,0,1:T(8,128)}, s32[]{:T(128)}) %tuple.626), condition=%wide.while_cond.clone.8, body=%wide.while_body.clone.8.sunk | while | flops 2 | bytes 411249 | solution.py:70
  229.8 6.6 %while.73 = (s32[]{:T(128)}, f32[2,2,9,4096]{3,2,1,0:T(8,128)S(1)}, s32[2,4]{1,0:T(2,128)}, f32[2,2,9,2048]{3,2,0,1:T(8,128)}, s32[]{:T(128)}) while((s32[]{:T(128)}, f32[2,2,9,4096]{3,2,1,0:T(8,128)S(1)}, s32[2,4]{1,0:T(2,128)}, f32[2,2,9,2048]{3,2,0,1:T(8,128)}, s32[]{:T(128)}) %tuple.571), condition=%wide.while_cond.clone.13, body=%wide.while_body.clone.13.sunk | while | flops 2 | bytes 411249 | solution.py:69
  237.2 7.0 %while.74 = (s32[]{:T(128)}, f32[2,2,9,4096]{3,2,1,0:T(8,128)S(1)}, s32[2,4]{1,0:T(2,128)}, f32[2,2,9,2048]{3,2,0,1:T(8,128)}, s32[]{:T(128)}) while((s32[]{:T(128)}, f32[2,2,9,4096]{3,2,1,0:T(8,128)S(1)}, s32[2,4]{1,0:T(2,128)}, f32[2,2,9,2048]{3,2,0,1:T(8,128)}, s32[]{:T(128)}) %tuple.627), condition=%wide.while_cond.clone.14, body=%wide.while_body.clone.14.sunk | while | flops 2 | bytes 411249 | solution.py:70
  245.0 5.2 %multiply_reduce_fusion.2 = (f32[]{:T(128)}, f32[2,2,8,2048]{3,2,1,0:T(8,128)S(1)}) fusion(f32[2,8,2048]{2,1,0:T(8,128)S(1)} %subtract_convert_fusion, f32[1,2,8,2048]{3,2,1,0:T(8,128)} %get-tuple-element.912, f32[1,2,8,2048]{3,2,1,0:T(8,128)} %get-tuple-element.911, f32[2,2,9,2048]{3,2,0,1:T(8,128)} %get-tuple-element.188, ...), kind=kLoop, calls=%fused_computation.199 | loop fusion | flops 5308415 | bytes 8851492 | tf_op jit(solution)/shard_map/reduce_sum | solution.py:115
  250.2 48.9 %all-reduce.2 = (f32[]{:T(128)}, f32[]{:T(128)}) all-reduce(f32[]{:T(128)} %get-tuple-element.833, f32[]{:T(128)} %get-tuple-element.831), channel_id=1, replica_groups=mesh['sec'=8,'tile'=4] {'sec','tile'}, use_global_device_ids=true, to_apply=%region_8.10 | all-reduce | flops 2 | bytes 16 | tf_op jit(solution)/shard_map/psum | solution.py:115
  306.4 4.4 collective-permute-done.9
  322.5 6.6 %while.77 = (s32[]{:T(128)}, f32[2,2,9,4096]{3,2,1,0:T(8,128)S(1)}, s32[2,4]{1,0:T(2,128)}, f32[2,2,9,2048]{3,2,0,1:T(8,128)}, s32[]{:T(128)}) while((s32[]{:T(128)}, f32[2,2,9,4096]{3,2,1,0:T(8,128)S(1)}, s32[2,4]{1,0:T(2,128)}, f32[2,2,9,2048]{3,2,0,1:T(8,128)}, s32[]{:T(128)}) %tuple.644), condition=%wide.while_cond.clone.17, body=%wide.while_body.clone.17.sunk | while | flops 2 | bytes 411405 | solution.py:69
  329.9 6.8 %while.78 = (s32[]{:T(128)}, f32[2,2,9,4096]{3,2,1,0:T(8,128)S(1)}, s32[2,4]{1,0:T(2,128)}, f32[2,2,9,2048]{3,2,0,1:T(8,128)}, s32[]{:T(128)}) while((s32[]{:T(128)}, f32[2,2,9,4096]{3,2,1,0:T(8,128)S(1)}, s32[2,4]{1,0:T(2,128)}, f32[2,2,9,2048]{3,2,0,1:T(8,128)}, s32[]{:T(128)}) %tuple.642), condition=%wide.while_cond.clone.18, body=%wide.while_body.clone.18.sunk | while | flops 2 | bytes 411405 | solution.py:70
  340.5 6.7 %while.79 = (s32[]{:T(128)}, f32[2,2,9,4096]{3,2,1,0:T(8,128)S(1)}, s32[2,4]{1,0:T(2,128)}, f32[2,2,9,2048]{3,2,0,1:T(8,128)}, s32[]{:T(128)}) while((s32[]{:T(128)}, f32[2,2,9,4096]{3,2,1,0:T(8,128)S(1)}, s32[2,4]{1,0:T(2,128)}, f32[2,2,9,2048]{3,2,0,1:T(8,128)}, s32[]{:T(128)}) %tuple.640), condition=%wide.while_cond.clone.19, body=%wide.while_body.clone.19.sunk | while | flops 2 | bytes 411405 | solution.py:69
  348.0 6.5 %while.80 = (s32[]{:T(128)}, f32[2,2,9,4096]{3,2,1,0:T(8,128)S(1)}, s32[2,4]{1,0:T(2,128)}, f32[2,2,9,2048]{3,2,0,1:T(8,128)}, s32[]{:T(128)}) while((s32[]{:T(128)}, f32[2,2,9,4096]{3,2,1,0:T(8,128)S(1)}, s32[2,4]{1,0:T(2,128)}, f32[2,2,9,2048]{3,2,0,1:T(8,128)}, s32[]{:T(128)}) %tuple.638), condition=%wide.while_cond.clone.20, body=%wide.while_body.clone.20.sunk | while | flops 2 | bytes 411405 | solution.py:70
  358.3 6.3 %while.75 = (s32[]{:T(128)}, f32[2,2,9,4096]{3,2,1,0:T(8,128)S(1)}, s32[2,4]{1,0:T(2,128)}, f32[2,2,9,2048]{3,2,0,1:T(8,128)}, s32[]{:T(128)}) while((s32[]{:T(128)}, f32[2,2,9,4096]{3,2,1,0:T(8,128)S(1)}, s32[2,4]{1,0:T(2,128)}, f32[2,2,9,2048]{3,2,0,1:T(8,128)}, s32[]{:T(128)}) %tuple.636), condition=%wide.while_cond.clone.15, body=%wide.while_body.clone.15.sunk | while | flops 2 | bytes 411405 | solution.py:69
  365.4 6.5 %while.76 = (s32[]{:T(128)}, f32[2,2,9,4096]{3,2,1,0:T(8,128)S(1)}, s32[2,4]{1,0:T(2,128)}, f32[2,2,9,2048]{3,2,0,1:T(8,128)}, s32[]{:T(128)}) while((s32[]{:T(128)}, f32[2,2,9,4096]{3,2,1,0:T(8,128)S(1)}, s32[2,4]{1,0:T(2,128)}, f32[2,2,9,2048]{3,2,0,1:T(8,128)}, s32[]{:T(128)}) %tuple.634), condition=%wide.while_cond.clone.16, body=%wide.while_body.clone.16.sunk | while | flops 2 | bytes 411405 | solution.py:70
  375.7 6.7 %while.81 = (s32[]{:T(128)}, f32[2,2,9,4096]{3,2,1,0:T(8,128)S(1)}, s32[2,4]{1,0:T(2,128)}, f32[2,2,9,2048]{3,2,0,1:T(8,128)}, s32[]{:T(128)}) while((s32[]{:T(128)}, f32[2,2,9,4096]{3,2,1,0:T(8,128)S(1)}, s32[2,4]{1,0:T(2,128)}, f32[2,2,9,2048]{3,2,0,1:T(8,128)}, s32[]{:T(128)}) %tuple.632), condition=%wide.while_cond.clone.21, body=%wide.while_body.clone.21.sunk | while | flops 2 | bytes 411405 | solution.py:69
  383.2 6.6 %while.82 = (s32[]{:T(128)}, f32[2,2,9,4096]{3,2,1,0:T(8,128)S(1)}, s32[2,4]{1,0:T(2,128)}, f32[2,2,9,2048]{3,2,0,1:T(8,128)}, s32[]{:T(128)}) while((s32[]{:T(128)}, f32[2,2,9,4096]{3,2,1,0:T(8,128)S(1)}, s32[2,4]{1,0:T(2,128)}, f32[2,2,9,2048]{3,2,0,1:T(8,128)}, s32[]{:T(128)}) %tuple.630), condition=%wide.while_cond.clone.22, body=%wide.while_body.clone.22.sunk | while | flops 2 | bytes 411405 | solution.py:70
  390.6 5.2 %multiply_reduce_fusion = (f32[]{:T(128)}, f32[2,2,8,2048]{3,2,1,0:T(8,128)S(1)}) fusion(f32[2,8,2048]{2,1,0:T(8,128)S(1)} %subtract_convert_fusion, f32[1,2,8,2048]{3,2,1,0:T(8,128)} %get-tuple-element.912, f32[1,2,8,2048]{3,2,1,0:T(8,128)} %get-tuple-element.911, f32[2,2,9,2048]{3,2,0,1:T(8,128)} %get-tuple-element.196, ...), kind=kLoop, calls=%fused_computation.195 | loop fusion | flops 5308415 | bytes 8851492 | tf_op jit(solution)/shard_map/reduce_sum | solution.py:115
  395.8 47.5 %all-reduce.1 = (f32[]{:T(128)}, f32[]{:T(128)}) all-reduce(f32[]{:T(128)} %get-tuple-element.829, f32[]{:T(128)} %get-tuple-element.827), channel_id=1, replica_groups=mesh['sec'=8,'tile'=4] {'sec','tile'}, use_global_device_ids=true, to_apply=%region_12.14 | all-reduce | flops 2 | bytes 16 | tf_op jit(solution)/shard_map/psum | solution.py:115
  (477 shorter events, 264.8 us)
Async XLA Ops:
  0.6 10.8 %copy-start.1 = (bf16[2,4,2,8,2048]{4,3,2,1,0:T(8,128)(2,1)S(1)}, bf16[2,4,2,8,2048]{4,3,2,1,0:T(8,128)(2,1)}, u32[]{:S(2)}) copy-start(bf16[2,4,2,8,2048]{4,3,2,1,0:T(8,128)(2,1)} %param.12) | copy-start | bytes 1572868
  1.8 31.3 %collective-permute-start = (f32[2,2,3,2048]{3,2,1,0:T(4,128)S(1)}, f32[2,2,3,2048]{3,2,1,0:T(4,128)S(1)}, u32[]{:S(2)}, u32[]{:S(2)}) collective-permute-start(f32[2,2,3,2048]{3,2,1,0:T(4,128)S(1)} %get-tuple-element.932), channel_id=1, source_target_pairs={{0,1},{1,2},{2,3},{4,5},{5,6},{6,7},{8,9},{9,10},{10,11},{12,13},{... | collective-permute-start | bytes 294920 | tf_op jit(solution)/shard_map/ppermute | solution.py:34
  6.7 27.0 %collective-permute-start.1 = (f32[2,2,3,2048]{3,2,1,0:T(4,128)S(1)}, f32[2,2,3,2048]{3,2,1,0:T(4,128)S(1)}, u32[]{:S(2)}, u32[]{:S(2)}) collective-permute-start(f32[2,2,3,2048]{3,2,1,0:T(4,128)S(1)} %get-tuple-element.931), channel_id=1, source_target_pairs={{1,0},{2,1},{3,2},{5,4},{6,5},{7,6},{9,8},{10,9},{11,10},{13,12},{... | collective-permute-start | bytes 294920 | tf_op jit(solution)/shard_map/ppermute | solution.py:36
  12.2 87.2 %copy-start.2 = (f32[2,8,2048]{2,1,0:T(8,128)}, f32[2,8,2048]{2,1,0:T(8,128)S(1)}, u32[]{:S(2)}) copy-start(f32[2,8,2048]{2,1,0:T(8,128)S(1)} %get-tuple-element.892) | copy-start | bytes 393220
  12.2 87.2 %copy-start.4 = (f32[2,8,2048]{2,1,0:T(8,128)}, f32[2,8,2048]{2,1,0:T(8,128)S(1)}, u32[]{:S(2)}) copy-start(f32[2,8,2048]{2,1,0:T(8,128)S(1)} %get-tuple-element.893) | copy-start | bytes 393220
  14.4 14.7 %copy-start.32 = (s32[2,8,2048]{2,1,0:T(8,128)S(1)}, s32[2,8,2048]{2,1,0:T(8,128)}, u32[]{:S(2)}) copy-start(s32[2,8,2048]{2,1,0:T(8,128)} %param.14) | copy-start | bytes 393220
  15.7 13.4 %copy-start.26 = (f32[2,2,8,2048]{3,2,1,0:T(8,128)S(1)}, f32[2,2,8,2048]{3,2,1,0:T(8,128)}, u32[]{:S(2)}) copy-start(f32[2,2,8,2048]{3,2,1,0:T(8,128)} %param.11) | copy-start | bytes 786436
  33.8 4.5 %collective-permute-start.2 = (f32[2,2,14,2048]{3,0,1,2:T(2,128)S(1)}, f32[2,2,14,2048]{3,0,1,2:T(2,128)S(1)}, u32[]{:S(2)}, u32[]{:S(2)}) collective-permute-start(f32[2,2,14,2048]{3,0,1,2:T(2,128)S(1)} %copy_dynamic-update-slice_fusion.1), channel_id=1, source_target_pairs={{0,4},{4,8},{8,12},{12,16},{16,20},{20,24},{24,28},{1,5},{5,9},{9,... | collective-permute-start | bytes 1376264 | tf_op jit(solution)/shard_map/ppermute | solution.py:34
  36.1 4.5 %collective-permute-start.3 = (f32[2,2,14,2048]{3,0,1,2:T(2,128)S(1)}, f32[2,2,14,2048]{3,0,1,2:T(2,128)S(1)}, u32[]{:S(2)}, u32[]{:S(2)}) collective-permute-start(f32[2,2,14,2048]{3,0,1,2:T(2,128)S(1)} %copy_dynamic-update-slice_fusion.1), channel_id=1, source_target_pairs={{4,0},{8,4},{12,8},{16,12},{20,16},{24,20},{28,24},{5,1},{9,5},{13... | collective-permute-start | bytes 1376264 | tf_op jit(solution)/shard_map/ppermute | solution.py:36
  88.9 10.5 %copy-start.14 = (f32[2,8,2048]{2,1,0:T(8,128)S(1)}, f32[2,8,2048]{2,1,0:T(8,128)}, u32[]{:S(2)}) copy-start(f32[2,8,2048]{2,1,0:T(8,128)} %get-tuple-element.902) | copy-start | bytes 393220
  88.9 10.5 %copy-start.15 = (f32[2,8,2048]{2,1,0:T(8,128)S(1)}, f32[2,8,2048]{2,1,0:T(8,128)}, u32[]{:S(2)}) copy-start(f32[2,8,2048]{2,1,0:T(8,128)} %get-tuple-element.903) | copy-start | bytes 393220
  92.8 6.7 %copy-start.10 = (f32[2,8,2048]{2,1,0:T(8,128)S(1)}, f32[2,8,2048]{2,1,0:T(8,128)}, u32[]{:S(2)}) copy-start(f32[2,8,2048]{2,1,0:T(8,128)} %get-tuple-element.898) | copy-start | bytes 393220
  92.8 6.7 %copy-start.11 = (f32[2,8,2048]{2,1,0:T(8,128)S(1)}, f32[2,8,2048]{2,1,0:T(8,128)}, u32[]{:S(2)}) copy-start(f32[2,8,2048]{2,1,0:T(8,128)} %get-tuple-element.899) | copy-start | bytes 393220
  92.8 6.7 %copy-start.12 = (f32[2,8,2048]{2,1,0:T(8,128)S(1)}, f32[2,8,2048]{2,1,0:T(8,128)}, u32[]{:S(2)}) copy-start(f32[2,8,2048]{2,1,0:T(8,128)} %get-tuple-element.900) | copy-start | bytes 393220
  92.8 6.7 %copy-start.13 = (f32[2,8,2048]{2,1,0:T(8,128)S(1)}, f32[2,8,2048]{2,1,0:T(8,128)}, u32[]{:S(2)}) copy-start(f32[2,8,2048]{2,1,0:T(8,128)} %get-tuple-element.901) | copy-start | bytes 393220
  93.8 5.8 %copy-start.8 = (f32[2,8,2048]{2,1,0:T(8,128)S(1)}, f32[2,8,2048]{2,1,0:T(8,128)}, u32[]{:S(2)}) copy-start(f32[2,8,2048]{2,1,0:T(8,128)} %get-tuple-element.896) | copy-start | bytes 393220
  93.8 5.8 %copy-start.9 = (f32[2,8,2048]{2,1,0:T(8,128)S(1)}, f32[2,8,2048]{2,1,0:T(8,128)}, u32[]{:S(2)}) copy-start(f32[2,8,2048]{2,1,0:T(8,128)} %get-tuple-element.897) | copy-start | bytes 393220
  100.2 54.8 %copy-start.27 = (f32[2,2,8,2048]{3,2,1,0:T(8,128)S(1)}, f32[2,2,8,2048]{3,2,1,0:T(8,128)}, u32[]{:S(2)}) copy-start(f32[2,2,8,2048]{3,2,1,0:T(8,128)} %param.11) | copy-start | bytes 786436
  155.8 5.9 %collective-permute-start.4 = (f32[2,2,3,2048]{3,2,1,0:T(4,128)S(1)}, f32[2,2,3,2048]{3,2,1,0:T(4,128)S(1)}, u32[]{:S(2)}, u32[]{:S(2)}) collective-permute-start(f32[2,2,3,2048]{3,2,1,0:T(4,128)S(1)} %get-tuple-element.925), channel_id=1, source_target_pairs={{0,1},{1,2},{2,3},{4,5},{5,6},{6,7},{8,9},{9,10},{10,11},{12,13},{... | collective-permute-start | bytes 294920 | tf_op jit(solution)/shard_map/ppermute | solution.py:34
  159.2 6.9 %collective-permute-start.5 = (f32[2,2,3,2048]{3,2,1,0:T(4,128)S(1)}, f32[2,2,3,2048]{3,2,1,0:T(4,128)S(1)}, u32[]{:S(2)}, u32[]{:S(2)}) collective-permute-start(f32[2,2,3,2048]{3,2,1,0:T(4,128)S(1)} %get-tuple-element.926), channel_id=1, source_target_pairs={{1,0},{2,1},{3,2},{5,4},{6,5},{7,6},{9,8},{10,9},{11,10},{13,12},{... | collective-permute-start | bytes 294920 | tf_op jit(solution)/shard_map/ppermute | solution.py:36
  161.7 12.1 %copy-start.24 = (f32[2,2,3,2048]{3,2,1,0:T(4,128)}, f32[2,2,3,2048]{3,2,1,0:T(4,128)S(1)}, u32[]{:S(2)}) copy-start(f32[2,2,3,2048]{3,2,1,0:T(4,128)S(1)} %collective-permute-done.4) | copy-start | bytes 294916
  166.0 7.7 %copy-start.25 = (f32[2,2,3,2048]{3,2,1,0:T(4,128)}, f32[2,2,3,2048]{3,2,1,0:T(4,128)S(1)}, u32[]{:S(2)}) copy-start(f32[2,2,3,2048]{3,2,1,0:T(4,128)S(1)} %collective-permute-done.5) | copy-start | bytes 294916
  166.1 3.7 collective-permute-start.6
  167.5 6.3 %collective-permute-start.7 = (f32[2,2,14,2048]{3,2,1,0:T(8,128)S(1)}, f32[2,2,14,2048]{3,2,1,0:T(8,128)S(1)}, u32[]{:S(2)}, u32[]{:S(2)}) collective-permute-start(f32[2,2,14,2048]{3,2,1,0:T(8,128)S(1)} %pad_maximum_fusion.24), channel_id=1, source_target_pairs={{4,0},{8,4},{12,8},{16,12},{20,16},{24,20},{28,24},{5,1},{9,5},{13... | collective-permute-start | bytes 1376264 | tf_op jit(solution)/shard_map/ppermute | solution.py:36
  237.2 7.0 %copy-start.3 = (f32[2,8,2048]{2,1,0:T(8,128)S(1)}, f32[2,8,2048]{2,1,0:T(8,128)}, u32[]{:S(2)}) copy-start(f32[2,8,2048]{2,1,0:T(8,128)} %copy-done.2) | copy-start | bytes 393220
  237.2 7.0 %copy-start.5 = (f32[2,8,2048]{2,1,0:T(8,128)S(1)}, f32[2,8,2048]{2,1,0:T(8,128)}, u32[]{:S(2)}) copy-start(f32[2,8,2048]{2,1,0:T(8,128)} %copy-done.4) | copy-start | bytes 393220
  301.3 5.1 %collective-permute-start.8 = (f32[2,2,3,2048]{3,2,1,0:T(4,128)S(1)}, f32[2,2,3,2048]{3,2,1,0:T(4,128)S(1)}, u32[]{:S(2)}, u32[]{:S(2)}) collective-permute-start(f32[2,2,3,2048]{3,2,1,0:T(4,128)S(1)} %get-tuple-element.919), channel_id=1, source_target_pairs={{0,1},{1,2},{2,3},{4,5},{5,6},{6,7},{8,9},{9,10},{10,11},{12,13},{... | collective-permute-start | bytes 294920 | tf_op jit(solution)/shard_map/ppermute | solution.py:34
  303.9 6.9 %collective-permute-start.9 = (f32[2,2,3,2048]{3,2,1,0:T(4,128)S(1)}, f32[2,2,3,2048]{3,2,1,0:T(4,128)S(1)}, u32[]{:S(2)}, u32[]{:S(2)}) collective-permute-start(f32[2,2,3,2048]{3,2,1,0:T(4,128)S(1)} %get-tuple-element.920), channel_id=1, source_target_pairs={{1,0},{2,1},{3,2},{5,4},{6,5},{7,6},{9,8},{10,9},{11,10},{13,12},{... | collective-permute-start | bytes 294920 | tf_op jit(solution)/shard_map/ppermute | solution.py:36
  306.3 12.1 %copy-start.22 = (f32[2,2,3,2048]{3,2,1,0:T(4,128)}, f32[2,2,3,2048]{3,2,1,0:T(4,128)S(1)}, u32[]{:S(2)}) copy-start(f32[2,2,3,2048]{3,2,1,0:T(4,128)S(1)} %collective-permute-done.8) | copy-start | bytes 294916
  310.7 7.7 %copy-start.23 = (f32[2,2,3,2048]{3,2,1,0:T(4,128)}, f32[2,2,3,2048]{3,2,1,0:T(4,128)S(1)}, u32[]{:S(2)}) copy-start(f32[2,2,3,2048]{3,2,1,0:T(4,128)S(1)} %collective-permute-done.9) | copy-start | bytes 294916
  310.8 3.7 collective-permute-start.10
  312.1 6.3 %collective-permute-start.11 = (f32[2,2,14,2048]{3,2,1,0:T(8,128)S(1)}, f32[2,2,14,2048]{3,2,1,0:T(8,128)S(1)}, u32[]{:S(2)}, u32[]{:S(2)}) collective-permute-start(f32[2,2,14,2048]{3,2,1,0:T(8,128)S(1)} %pad_maximum_fusion.25), channel_id=1, source_target_pairs={{4,0},{8,4},{12,8},{16,12},{20,16},{24,20},{28,24},{5,1},{9,5},{13... | collective-permute-start | bytes 1376264 | tf_op jit(solution)/shard_map/ppermute | solution.py:36
  (67 other events, 82.7 us)
where the time goes:
time: 448 us; the launch traced here: 445 us
  local copies, waits for them, and re-layouts  209 us (47%)
  blocking collectives  153 us (34%)
  other arithmetic  33.1 us (7%)
  starting transfers between devices  24 us (5%)
  waiting for transfers between devices  20.1 us (4%)
  between operations  5.67 us (1%)
    psum x3, blocking collectives, shards(): lax.psum((jnp.sum(force * force), jnp.sum(moving * moving)), ('sec', 'til...  145 us
    another operation x113, local copies, waits for them, and re-layouts, pull(): first = jnp.roll(part_rows, -shift[1], axis=2)  90.8 us
    another operation x76, local copies, waits for them, and re-layouts, pull(): second = jnp.roll(part_rows, -shift[1] - 1, axis=2)  71.8 us
    ppermute x6, waiting for transfers between devices, padded(): lax.ppermute(head, axis, [((i + 1) % count, i) for i in range(ends)])  18.9 us
    ppermute x6, starting transfers between devices, padded(): lax.ppermute(tail, axis, [(i, (i + 1) % count) for i in range(ends)])  15.8 us
    reduce_sum x3, other arithmetic, shards(): jnp.sum(force * force)  15.6 us
    gather x40, local copies, waits for them, and re-layouts  12.7 us
    gather x12, local copies, waits for them, and re-layouts, pull(): part_rows = lax.dynamic_slice_in_dim(block, 3 + shift[0], height + 1, 1)  10.4 us
  transfers between devices with their start and end apart: 12, of which 7 were waited for; matrix products, arithmetic and copies ran while one was open for 4% of the time, Pallas kernels for 0%

commit v1 on v0

v1 whole, which is shorter than its diff:
```python
import functools

import jax
import jax.numpy as jnp
from jax import lax
from jax.experimental import pallas as pl
from jax.experimental.pallas import tpu as pltpu
from jax.sharding import PartitionSpec as P

ITERS = 3
LANES = 128
UP = 2
DOWN = 3
REACH = 2

in_stiff = 1.0
anchor_stiff = 0.25
cross_stiff = (0.25, 0.5, 0.5, 0.25)
reaches = (-2, -1, 1, 2)
MESH = pl.DeviceIdType.MESH


def pick(step, values):
    chosen = jnp.float32(values[-1])
    for index in range(len(values) - 1):
        chosen = jnp.where(step == index, jnp.float32(values[index]), chosen)
    return chosen


def kernel(
    n_sec, n_tile, off_ref, u_ref, v_in, frac_ref, fixed_ref, trans_ref, u_out, v_out,
    ext, force, keep, trans_all, anchor, part, part_tile, norms_sec, norms_tile,
    halo_send, halo_recv, tr_send, tr_recv, sec_send, sec_recv, tile_send, tile_recv,
):
    _, count, height, subs, lanes = u_ref.shape
    width = subs * lanes
    sections = count * n_sec
    rows = height * n_tile
    my_sec = lax.axis_index("sec")
    my_tile = lax.axis_index("tile")
    sec_first = my_sec * count
    row_first = my_tile * height
    shape = (height, subs, lanes)
    grow = row_first + lax.broadcasted_iota(jnp.int32, shape, 0)
    lane = lax.broadcasted_iota(jnp.int32, shape, 2)
    gcol = lax.broadcasted_iota(jnp.int32, shape, 1) * lanes + lane
    lane_of = lax.broadcasted_iota(jnp.int32, (1, 1, lanes), 2)

    ways = [(a, b) for a in (-1, 0, 1) for b in (-1, 0, 1) if (a, b) != (0, 0)]
    sec_at = {-1: pl.ds(REACH + count, REACH), 0: pl.ds(REACH, count), 1: pl.ds(0, REACH)}
    sec_from = {-1: pl.ds(REACH, REACH), 0: pl.ds(REACH, count), 1: pl.ds(count, REACH)}
    row_at = {-1: pl.ds(UP + height, DOWN), 0: pl.ds(UP, height), 1: pl.ds(0, UP)}
    row_from = {-1: pl.ds(UP, DOWN), 0: pl.ds(UP, height), 1: pl.ds(height, UP)}

    def halo(way):
        a, b = ways[way]
        return pltpu.make_async_remote_copy(
            src_ref=ext.at[:, sec_from[a], row_from[b]],
            dst_ref=ext.at[:, sec_at[a], row_at[b]],
            send_sem=halo_send.at[way],
            recv_sem=halo_recv.at[way],
            device_id=(lax.rem(my_sec + a + n_sec, n_sec), lax.rem(my_tile + b + n_tile, n_tile)),
            device_id_type=MESH,
        )

    def there(a, b):
        sec_ok = (my_sec + a >= 0) & (my_sec + a < n_sec)
        return sec_ok & (my_tile + b >= 0) & (my_tile + b < n_tile)

    def send_halo():
        for way, (a, b) in enumerate(ways):
            pl.when(there(a, b))(lambda way=way: halo(way).start())

    def halo_sent():
        for way, (a, b) in enumerate(ways):
            pl.when(there(a, b))(lambda way=way: halo(way).wait_send())

    def halo_here():
        for way, (a, b) in enumerate(ways):
            pl.when(there(-a, -b))(lambda way=way: halo(way).wait_recv())

    def spread(src, slots, send, recv, n, me, peer):
        def copy(turn, place):
            return pltpu.make_async_remote_copy(
                src_ref=src,
                dst_ref=slots.at[place],
                send_sem=send.at[turn],
                recv_sem=recv.at[place],
                device_id=peer(lax.rem(me + turn, n)),
                device_id_type=MESH,
            )

        for turn in range(1, n):
            copy(turn, me).start()
        return copy

    def gathered(copy, n, me):
        for turn in range(1, n):
            copy(turn, lax.rem(me + turn, n)).wait_recv()
        for turn in range(1, n):
            copy(turn, me).wait_send()

    def along_sec(to):
        return (to, my_tile)

    def along_tile(to):
        return (my_sec, to)

    def shifted(cells, by):
        turned = pltpu.roll(cells, lax.rem(lanes - by, lanes), 2)
        after = pltpu.roll(turned, subs - 1, 1)
        before = pltpu.roll(turned, 1, 1)
        place = lane_of + by
        return jnp.where(place > lanes - 1, after, jnp.where(place < 0, before, turned))

    ext[:, REACH : REACH + count, UP : UP + height] = u_ref[...]
    send_halo()
    trans_copy = spread(trans_ref, trans_all, tr_send, tr_recv, n_sec, my_sec, along_sec)
    keep[...] = (1 - fixed_ref[...]).astype(jnp.float32)
    for c in range(2):
        v_out[c] = v_in[c] * keep[...]
    trans_all[my_sec] = trans_ref[...]
    gathered(trans_copy, n_sec, my_sec)
    before = jnp.zeros(trans_ref.shape, jnp.float32)
    for turn in range(n_sec):
        before = before + jnp.where(turn < my_sec, trans_all[turn], 0.0)
    for c in range(2):
        run = jnp.zeros((1, lanes), jnp.float32)
        for s in range(count):
            run = run + before[2 * s + c : 2 * s + c + 1]
        for s in range(count):
            run = run + trans_ref[2 * s + c : 2 * s + c + 1, :]
            anchor[2 * s + c : 2 * s + c + 1, :] = run

    def iteration(step, _):
        halo_here()
        ff = jnp.zeros((subs, lanes), jnp.float32)
        vv = jnp.zeros((subs, lanes), jnp.float32)
        for s in range(count):
            own = [ext[c, REACH + s, UP : UP + height] for c in range(2)]
            total = []
            for c in range(2):
                mid = own[c]
                above = ext[c, REACH + s, UP - 1 : UP - 1 + height]
                below = ext[c, REACH + s, UP + 1 : UP + 1 + height]
                f = jnp.where(grow > 0, above - mid, 0.0)
                f = f + jnp.where(grow < rows - 1, below - mid, 0.0)
                f = f + jnp.where(gcol > 0, shifted(mid, -1) - mid, 0.0)
                f = f + jnp.where(gcol < width - 1, shifted(mid, 1) - mid, 0.0)
                hold = anchor[2 * s + c : 2 * s + c + 1, :][None]
                total.append(in_stiff * f + anchor_stiff * (hold - mid))
            for j in range(4):
                reach = reaches[j]
                dr = off_ref[(j * count + s) * 2]
                dc = off_ref[(j * count + s) * 2 + 1]
                fr = frac_ref[0, j, s].astype(jnp.float32)
                fc = frac_ref[1, j, s].astype(jnp.float32)
                other = sec_first + s + reach
                least = jnp.where((other >= 0) & (other < sections), 0, rows + height)
                valid = (grow + dr >= least) & (grow + dr + 1 <= rows - 1)
                valid = valid & (gcol + dc >= 0) & (gcol + dc + 1 <= width - 1)
                flow = (dr.astype(jnp.float32) + fr, dc.astype(jnp.float32) + fc)
                for c in range(2):
                    near = ext[c, REACH + s + reach, pl.ds(UP + dr, height + 1)]
                    first = shifted(near, dc)
                    second = shifted(near, dc + 1)
                    top = first[:height] + fc * (second[:height] - first[:height])
                    low = first[1:] + fc * (second[1:] - first[1:])
                    match = top + fr * (low - top)
                    gap = match + flow[c] - own[c]
                    total[c] = total[c] + jnp.where(valid, cross_stiff[j] * gap, 0.0)
            for c in range(2):
                f = total[c] * keep[s]
                force[c, s] = f
                v = v_out[c, s]
                ff = ff + jnp.sum(f * f, 0)
                vv = vv + jnp.sum(v * v, 0)
        part[step, 0] = ff
        part[step, 1] = vv
        norms_sec[step, my_sec] = part[step]
        copy = spread(
            part.at[step], norms_sec.at[step], sec_send.at[step], sec_recv.at[step], n_sec, my_sec, along_sec
        )
        halo_sent()
        gathered(copy, n_sec, my_sec)
        summed = norms_sec[step, 0]
        for turn in range(1, n_sec):
            summed = summed + norms_sec[step, turn]
        part_tile[step] = summed
        norms_tile[step, my_tile] = summed
        copy = spread(
            part_tile.at[step], norms_tile.at[step], tile_send.at[step], tile_recv.at[step], n_tile, my_tile, along_tile
        )
        gathered(copy, n_tile, my_tile)
        summed = norms_tile[step, 0]
        for turn in range(1, n_tile):
            summed = summed + norms_tile[step, turn]
        all_ff = jnp.sum(summed[0], axis=(0, 1), keepdims=True)
        all_vv = jnp.sum(summed[1], axis=(0, 1), keepdims=True)
        ratio = jnp.sqrt(all_vv / (all_ff + 1e-06))
        alpha = pick(step, [0.1 * 0.99**k for k in range(ITERS)])
        delta = pick(step, [0.25 * 1.1**k for k in range(ITERS)])
        gain = jnp.broadcast_to(alpha * ratio + delta, (subs, lanes))[None]
        for c in range(2):
            for s in range(count):
                v = (1.0 - alpha) * v_out[c, s] + gain * force[c, s]
                v_out[c, s] = v
                u = ext[c, REACH + s, UP : UP + height] + delta * v
                ext[c, REACH + s, UP : UP + height] = u
        pl.when(step < ITERS - 1)(send_halo)
        return 0

    lax.fori_loop(0, ITERS, iteration, 0)
    u_out[...] = ext[:, REACH : REACH + count, UP : UP + height]


def shards(displacement, velocity, frac, offsets, fixed, trans):
    n_sec, n_tile = lax.axis_size("sec"), lax.axis_size("tile")
    _, count, height, width = displacement.shape
    subs = width // LANES
    cells = (2, count, height, subs, LANES)
    lines = -(-2 * count // 8) * 8
    shift = offsets[:, :, 0, :].reshape(-1)
    spread = jnp.broadcast_to(trans.reshape(-1, 1), (2 * count, LANES))
    spread = jnp.pad(spread, ((0, lines - 2 * count), (0, 0)))
    vmem = pl.BlockSpec(memory_space=pltpu.VMEM)
    dma = pltpu.SemaphoreType.DMA
    f32 = jnp.float32
    u, v = pl.pallas_call(
        functools.partial(kernel, n_sec, n_tile),
        out_shape=(jax.ShapeDtypeStruct(cells, f32), jax.ShapeDtypeStruct(cells, f32)),
        in_specs=[pl.BlockSpec(memory_space=pltpu.SMEM)] + [vmem] * 5,
        out_specs=(vmem, vmem),
        scratch_shapes=[
            pltpu.VMEM((2, count + 2 * REACH, height + UP + DOWN, subs, LANES), f32),
            pltpu.VMEM(cells, f32),
            pltpu.VMEM(cells[1:], f32),
            pltpu.VMEM((n_sec, lines, LANES), f32),
            pltpu.VMEM((lines, LANES), f32),
            pltpu.VMEM((ITERS, 2, subs, LANES), f32),
            pltpu.VMEM((ITERS, 2, subs, LANES), f32),
            pltpu.VMEM((ITERS, n_sec, 2, subs, LANES), f32),
            pltpu.VMEM((ITERS, n_tile, 2, subs, LANES), f32),
            dma((8,)),
            dma((8,)),
            dma((n_sec,)),
            dma((n_sec,)),
            dma((ITERS, n_sec)),
            dma((ITERS, n_sec)),
            dma((ITERS, n_tile)),
            dma((ITERS, n_tile)),
        ],
        compiler_params=pltpu.CompilerParams(has_side_effects=True, vmem_limit_bytes=40 * 2**20),
    )(
        shift,
        displacement.reshape(cells),
        velocity.reshape(cells),
        frac.reshape((2, 4) + cells[1:]),
        fixed.reshape(cells[1:]),
        spread,
    )
    return u.reshape(displacement.shape), v.reshape(displacement.shape)


def solution(mesh):
    placed = (
        P(None, "sec", "tile", None),
        P(None, "sec", "tile", None),
        P(None, None, "sec", "tile", None),
        P(None, "sec", "tile", None),
        P("sec", "tile", None),
        P("sec", None),
    )
    return jax.shard_map(
        shards,
        mesh=mesh,
        in_specs=placed,
        out_specs=(P(None, "sec", "tile", None), P(None, "sec", "tile", None)),
        check_vma=False,
    )
```

time: 448 us -> 72.4 us (0.16)
  local copies, waits for them, and re-layouts: 209 us -> 5.35 us
  blocking collectives: 153 us -> 0 us
  Pallas kernels: 0 us -> 66.1 us
  other arithmetic: 33.1 us -> 0 us
  starting transfers between devices: 24 us -> 0 us
  waiting for transfers between devices: 20.1 us -> 0 us
  between operations: 5.67 us -> 0.7 us
    another operation x190 -> x1, local copies, waits for them, and re-layouts: 163 us -> 0.09 us  [shards(): shift = offsets[:, :, 0, :].reshape(-1)]
    psum x3 -> x0, blocking collectives: 145 us -> none  [shards(): lax.psum((jnp.sum(force * force), jnp.sum(moving * moving)), ('sec', 'til...]
    pallas_call x0 -> x1, Pallas kernels: none -> 66.1 us  [shards(): pl.pallas_call(functools.partial(kernel, n_sec, n_tile), out_shape=(jax.S...]
    ppermute x12 -> x0, starting transfers between devices: 24 us -> none  [the longest x6 15.8 us: padded(): lax.ppermute(tail, axis, [(i, (i + 1) % count) for i in range(ends)])]
    gather x52 -> x0, local copies, waits for them, and re-layouts: 23.1 us -> none
    ppermute x12 -> x0, waiting for transfers between devices: 20.1 us -> none  [the longest x6 18.9 us: padded(): lax.ppermute(head, axis, [((i + 1) % count, i) for i in range(ends)])]
    reduce_sum x6 -> x0, other arithmetic: 17.7 us -> none  [the longest x3 15.6 us: shards(): jnp.sum(force * force)]
    transpose x8 -> x0, local copies, waits for them, and re-layouts: 9.1 us -> none  [pull(): part_rows = lax.dynamic_slice_in_dim(block, 3 + shift[0], height + 1, 1)]
  transfers between devices with their start and end apart: 12 -> 0, of which waited for: 7 -> 0; matrix products, arithmetic and copies ran while one was open for 4% -> 0% of each run, Pallas kernels for 0% -> 0%
where the time goes in v1:
time: 72.4 us; the launch traced here: 72.2 us
  Pallas kernels  66.1 us (91%)
  local copies, waits for them, and re-layouts  5.35 us (7%)
    pallas_call x1, Pallas kernels, shards(): pl.pallas_call(functools.partial(kernel, n_sec, n_tile), out_shape=(jax.S...  66.1 us
    unnamed x11, local copies, waits for them, and re-layouts  2.88 us
    reshape x2, local copies, waits for them, and re-layouts, shards(): return (u.reshape(displacement.shape), v.reshape(displacement.shape))  1.5 us

profile of v1, /device:TPU:0, one launch (start us, length us, event | category | flops | bytes accessed | tf_op | source)
XLA Modules:
  0.0 72.2 jit_solution(5427047456815730361)
XLA Ops:
  0.6 0.0 copy-start.1
  0.6 0.8 %broadcast_in_dim.2 = f32[4]{0:T(128)S(1)} reshape(f32[2,2]{1,0:T(2,128)} %param.11) | data formatting | bytes 32 | tf_op jit(solution)/shard_map/broadcast_in_dim | solution.py:224
  1.4 0.1 pad.7.trans_ref
  1.5 0.8 %copy.9 = s32[4,2,1,2]{3,1,0,2:T(2,128)S(1)} copy(s32[4,2,1,2]{0,3,2,1:T(2,128)} %param.9) | data formatting | bytes 128 | tf_op args[3]
  2.3 0.1 reshape_squeeze.3.off_ref
  2.4 0.0 copy-start.2
  2.4 1.0 %copy.15 = s32[2,8,16,128]{3,2,1,0:T(8,128)S(1)} copy(s32[2,8,16,128]{3,1,2,0:T(8,128)} %bitcast.33) | data formatting | bytes 262144
  3.4 0.0 copy-done.1
  3.4 0.0 copy-start
  3.4 0.0 copy-done.2
  3.5 0.9 %copy-done = bf16[2,4,2,8,2048]{4,3,2,1,0:T(8,128)(2,1)S(1)} copy-done((bf16[2,4,2,8,2048]{4,3,2,1,0:T(8,128)(2,1)S(1)}, bf16[2,4,2,8,2048]{4,3,2,1,0:T(8,128)(2,1)}, u32[]{:S(2)}) %copy-start) | copy-done | bytes 524312
  4.4 0.1 copy.12
  4.5 66.1 %shard_map.77 = (f32[2,2,8,16,128]{4,3,2,1,0:T(8,128)S(1)}, f32[2,2,8,16,128]{4,3,2,1,0:T(8,128)S(1)}) custom-call(s32[16]{0:T(128)S(1)} %reshape_squeeze.3.off_ref, f32[2,2,8,16,128]{4,3,2,1,0:T(8,128)S(1)} %bitcast.28, f32[2,2,8,16,128]{4,3,2,1,0:T(8,128)S(1)} %bitcast.29, bf16[2,4,2,8,16,128]{5,4,3,2,1,0:T(8,128)(2,1)S(1)} %bitcast.27, ...), custom_call_target="tpu_custom_call" | custom-call | tf_op jit(solution)/shard_map/pallas_call | solution.py:229
  70.7 0.7 %reshape.28 = f32[2,2,8,2048]{3,2,1,0:T(8,128)} reshape(f32[2,2,8,16,128]{4,3,2,1,0:T(8,128)S(1)} %get-tuple-element.4) | data formatting | bytes 524288 | tf_op jit(solution)/shard_map/reshape | solution.py:262
  71.4 0.7 %reshape.29 = f32[2,2,8,2048]{3,2,1,0:T(8,128)} reshape(f32[2,2,8,16,128]{4,3,2,1,0:T(8,128)S(1)} %get-tuple-element.5) | data formatting | bytes 524288 | tf_op jit(solution)/shard_map/reshape | solution.py:262
  (3 shorter events, 0.1 us)
Async XLA Ops:
  0.6 2.7 %copy-start.1 = (f32[2,2,8,2048]{3,2,1,0:T(8,128)S(1)}, f32[2,2,8,2048]{3,2,1,0:T(8,128)}, u32[]{:S(2)}) copy-start(f32[2,2,8,2048]{3,2,1,0:T(8,128)} %param.6) | copy-start | bytes 786436
  2.4 1.1 %copy-start.2 = (f32[2,2,8,2048]{3,2,1,0:T(8,128)S(1)}, f32[2,2,8,2048]{3,2,1,0:T(8,128)}, u32[]{:S(2)}) copy-start(f32[2,2,8,2048]{3,2,1,0:T(8,128)} %param.7) | copy-start | bytes 786436
  3.4 1.0 %copy-start = (bf16[2,4,2,8,2048]{4,3,2,1,0:T(8,128)(2,1)S(1)}, bf16[2,4,2,8,2048]{4,3,2,1,0:T(8,128)(2,1)}, u32[]{:S(2)}) copy-start(bf16[2,4,2,8,2048]{4,3,2,1,0:T(8,128)(2,1)} %param.8) | copy-start | bytes 1572868

commit v2 on v1

--- a/solution.py
+++ b/solution.py
@@ -29,7 +29,7 @@
 
 def kernel(
     n_sec, n_tile, off_ref, u_ref, v_in, frac_ref, fixed_ref, trans_ref, u_out, v_out,
-    ext, force, keep, trans_all, anchor, part, part_tile, norms_sec, norms_tile,
+    ext, ext_v, ext_f, keep, trans_all, anchor, part, part_tile, norms_sec, norms_tile,
     halo_send, halo_recv, tr_send, tr_recv, sec_send, sec_recv, tile_send, tile_recv,
 ):
     _, count, height, subs, lanes = u_ref.shape
@@ -52,13 +52,13 @@
     row_at = {-1: pl.ds(UP + height, DOWN), 0: pl.ds(UP, height), 1: pl.ds(0, UP)}
     row_from = {-1: pl.ds(UP, DOWN), 0: pl.ds(UP, height), 1: pl.ds(height, UP)}
 
-    def halo(way):
+    def halo(block, turn, way):
         a, b = ways[way]
         return pltpu.make_async_remote_copy(
-            src_ref=ext.at[:, sec_from[a], row_from[b]],
-            dst_ref=ext.at[:, sec_at[a], row_at[b]],
-            send_sem=halo_send.at[way],
-            recv_sem=halo_recv.at[way],
+            src_ref=block.at[:, sec_from[a], row_from[b]],
+            dst_ref=block.at[:, sec_at[a], row_at[b]],
+            send_sem=halo_send.at[turn, way],
+            recv_sem=halo_recv.at[turn, way],
             device_id=(lax.rem(my_sec + a + n_sec, n_sec), lax.rem(my_tile + b + n_tile, n_tile)),
             device_id_type=MESH,
         )
@@ -67,17 +67,17 @@
         sec_ok = (my_sec + a >= 0) & (my_sec + a < n_sec)
         return sec_ok & (my_tile + b >= 0) & (my_tile + b < n_tile)
 
-    def send_halo():
+    def send_halo(block, turn):
         for way, (a, b) in enumerate(ways):
-            pl.when(there(a, b))(lambda way=way: halo(way).start())
-
-    def halo_sent():
+            pl.when(there(a, b))(lambda way=way: halo(block, turn, way).start())
+
+    def halo_sent(block, turn):
         for way, (a, b) in enumerate(ways):
-            pl.when(there(a, b))(lambda way=way: halo(way).wait_send())
-
-    def halo_here():
+            pl.when(there(a, b))(lambda way=way: halo(block, turn, way).wait_send())
+
+    def halo_here(block, turn):
         for way, (a, b) in enumerate(ways):
-            pl.when(there(-a, -b))(lambda way=way: halo(way).wait_recv())
+            pl.when(there(-a, -b))(lambda way=way: halo(block, turn, way).wait_recv())
 
     def spread(src, slots, send, recv, n, me, peer):
         def copy(turn, place):
@@ -114,11 +114,12 @@
         return jnp.where(place > lanes - 1, after, jnp.where(place < 0, before, turned))
 
     ext[:, REACH : REACH + count, UP : UP + height] = u_ref[...]
-    send_halo()
+    send_halo(ext, 0)
     trans_copy = spread(trans_ref, trans_all, tr_send, tr_recv, n_sec, my_sec, along_sec)
     keep[...] = (1 - fixed_ref[...]).astype(jnp.float32)
     for c in range(2):
-        v_out[c] = v_in[c] * keep[...]
+        ext_v[c, REACH : REACH + count, UP : UP + height] = v_in[c] * keep[...]
+    send_halo(ext_v, 1)
     trans_all[my_sec] = trans_ref[...]
     gathered(trans_copy, n_sec, my_sec)
     before = jnp.zeros(trans_ref.shape, jnp.float32)
@@ -132,8 +133,9 @@
             run = run + trans_ref[2 * s + c : 2 * s + c + 1, :]
             anchor[2 * s + c : 2 * s + c + 1, :] = run
 
+    halo_here(ext, 0)
+
     def iteration(step, _):
-        halo_here()
         ff = jnp.zeros((subs, lanes), jnp.float32)
         vv = jnp.zeros((subs, lanes), jnp.float32)
         for s in range(count):
@@ -171,17 +173,30 @@
                     total[c] = total[c] + jnp.where(valid, cross_stiff[j] * gap, 0.0)
             for c in range(2):
                 f = total[c] * keep[s]
-                force[c, s] = f
-                v = v_out[c, s]
+                ext_f[step, c, REACH + s, UP : UP + height] = f
+                v = ext_v[c, REACH + s, UP : UP + height]
                 ff = ff + jnp.sum(f * f, 0)
                 vv = vv + jnp.sum(v * v, 0)
-        part[step, 0] = ff
-        part[step, 1] = vv
-        norms_sec[step, my_sec] = part[step]
+        line = lax.broadcasted_iota(jnp.int32, (8, lanes), 0)
+        ff = jnp.sum(ff, axis=0, keepdims=True)
+        vv = jnp.sum(vv, axis=0, keepdims=True)
+        mine = jnp.where(line == 0, ff, jnp.where(line == 1, vv, 0.0))
+        part[step] = mine
+        norms_sec[step, my_sec] = mine
         copy = spread(
             part.at[step], norms_sec.at[step], sec_send.at[step], sec_recv.at[step], n_sec, my_sec, along_sec
         )
-        halo_sent()
+
+        @pl.when(step < ITERS - 1)
+        def _():
+            send_halo(ext_f.at[step], 2 + step)
+
+        @pl.when(step == 0)
+        def _():
+            halo_sent(ext, 0)
+            halo_sent(ext_v, 1)
+            halo_here(ext_v, 1)
+
         gathered(copy, n_sec, my_sec)
         summed = norms_sec[step, 0]
         for turn in range(1, n_sec):
@@ -195,23 +210,31 @@
         summed = norms_tile[step, 0]
         for turn in range(1, n_tile):
             summed = summed + norms_tile[step, turn]
-        all_ff = jnp.sum(summed[0], axis=(0, 1), keepdims=True)
-        all_vv = jnp.sum(summed[1], axis=(0, 1), keepdims=True)
+        all_ff = jnp.sum(summed[0:1], axis=(0, 1), keepdims=True)
+        all_vv = jnp.sum(summed[1:2], axis=(0, 1), keepdims=True)
         ratio = jnp.sqrt(all_vv / (all_ff + 1e-06))
         alpha = pick(step, [0.1 * 0.99**k for k in range(ITERS)])
         delta = pick(step, [0.25 * 1.1**k for k in range(ITERS)])
         gain = jnp.broadcast_to(alpha * ratio + delta, (subs, lanes))[None]
-        for c in range(2):
-            for s in range(count):
-                v = (1.0 - alpha) * v_out[c, s] + gain * force[c, s]
-                v_out[c, s] = v
-                u = ext[c, REACH + s, UP : UP + height] + delta * v
-                ext[c, REACH + s, UP : UP + height] = u
-        pl.when(step < ITERS - 1)(send_halo)
+
+        @pl.when(step < ITERS - 1)
+        def _():
+            halo_here(ext_f.at[step], 2 + step)
+            halo_sent(ext_f.at[step], 2 + step)
+
+        def advance(place, _):
+            for c in range(2):
+                v = (1.0 - alpha) * ext_v[c, place] + gain * ext_f[step, c, place]
+                ext_v[c, place] = v
+                ext[c, place] = ext[c, place] + delta * v
+            return 0
+
+        lax.fori_loop(0, count + 2 * REACH, advance, 0)
         return 0
 
     lax.fori_loop(0, ITERS, iteration, 0)
     u_out[...] = ext[:, REACH : REACH + count, UP : UP + height]
+    v_out[...] = ext_v[:, REACH : REACH + count, UP : UP + height]
 
 
 def shards(displacement, velocity, frac, offsets, fixed, trans):
@@ -233,16 +256,17 @@
         out_specs=(vmem, vmem),
         scratch_shapes=[
             pltpu.VMEM((2, count + 2 * REACH, height + UP + DOWN, subs, LANES), f32),
-            pltpu.VMEM(cells, f32),
+            pltpu.VMEM((2, count + 2 * REACH, height + UP + DOWN, subs, LANES), f32),
+            pltpu.VMEM((ITERS, 2, count + 2 * REACH, height + UP + DOWN, subs, LANES), f32),
             pltpu.VMEM(cells[1:], f32),
             pltpu.VMEM((n_sec, lines, LANES), f32),
             pltpu.VMEM((lines, LANES), f32),
-            pltpu.VMEM((ITERS, 2, subs, LANES), f32),
-            pltpu.VMEM((ITERS, 2, subs, LANES), f32),
-            pltpu.VMEM((ITERS, n_sec, 2, subs, LANES), f32),
-            pltpu.VMEM((ITERS, n_tile, 2, subs, LANES), f32),
-            dma((8,)),
-            dma((8,)),
+            pltpu.VMEM((ITERS, 8, LANES), f32),
+            pltpu.VMEM((ITERS, 8, LANES), f32),
+            pltpu.VMEM((ITERS, n_sec, 8, LANES), f32),
+            pltpu.VMEM((ITERS, n_tile, 8, LANES), f32),
+            dma((1 + ITERS, 8)),
+            dma((1 + ITERS, 8)),
             dma((n_sec,)),
             dma((n_sec,)),
             dma((ITERS, n_sec)),

time: 72.4 us -> 67.9 us (0.938)
  Pallas kernels: 66.1 us -> 61.7 us
    pallas_call x1, Pallas kernels: 66.1 us -> 61.7 us  [shards(): pl.pallas_call(functools.partial(kernel, n_sec, n_tile), out_shape=(jax.S...]
where the time goes in v2:
time: 67.9 us; the launch traced here: 67.7 us
  Pallas kernels  61.7 us (91%)
  local copies, waits for them, and re-layouts  5.35 us (8%)
  between operations  0.7 us (1%)
    pallas_call x1, Pallas kernels, shards(): pl.pallas_call(functools.partial(kernel, n_sec, n_tile), out_shape=(jax.S...  61.7 us
    unnamed x11, local copies, waits for them, and re-layouts  2.88 us
    reshape x2, local copies, waits for them, and re-layouts, shards(): return (u.reshape(displacement.shape), v.reshape(displacement.shape))  1.5 us

profile of v2, /device:TPU:0, one launch (start us, length us, event | category | flops | bytes accessed | tf_op | source)
XLA Modules:
  0.0 67.7 jit_solution(10687674247077616635)
XLA Ops:
  0.6 0.0 copy-start.1
  0.6 0.8 %broadcast_in_dim.2 = f32[4]{0:T(128)S(1)} reshape(f32[2,2]{1,0:T(2,128)} %param.11) | data formatting | bytes 32 | tf_op jit(solution)/shard_map/broadcast_in_dim | solution.py:247
  1.4 0.1 pad.7.trans_ref
  1.5 0.8 %copy.9 = s32[4,2,1,2]{3,1,0,2:T(2,128)S(1)} copy(s32[4,2,1,2]{0,3,2,1:T(2,128)} %param.9) | data formatting | bytes 128 | tf_op args[3]
  2.3 0.1 reshape_squeeze.3.off_ref
  2.4 0.0 copy-start.2
  2.4 1.0 %copy.15 = s32[2,8,16,128]{3,2,1,0:T(8,128)S(1)} copy(s32[2,8,16,128]{3,1,2,0:T(8,128)} %bitcast.33) | data formatting | bytes 262144
  3.4 0.0 copy-done.1
  3.4 0.0 copy-start
  3.4 0.0 copy-done.2
  3.5 0.9 %copy-done = bf16[2,4,2,8,2048]{4,3,2,1,0:T(8,128)(2,1)S(1)} copy-done((bf16[2,4,2,8,2048]{4,3,2,1,0:T(8,128)(2,1)S(1)}, bf16[2,4,2,8,2048]{4,3,2,1,0:T(8,128)(2,1)}, u32[]{:S(2)}) %copy-start) | copy-done | bytes 524312
  4.4 0.1 copy.12
  4.5 61.7 %shard_map.77 = (f32[2,2,8,16,128]{4,3,2,1,0:T(8,128)S(1)}, f32[2,2,8,16,128]{4,3,2,1,0:T(8,128)S(1)}) custom-call(s32[16]{0:T(128)S(1)} %reshape_squeeze.3.off_ref, f32[2,2,8,16,128]{4,3,2,1,0:T(8,128)S(1)} %bitcast.28, f32[2,2,8,16,128]{4,3,2,1,0:T(8,128)S(1)} %bitcast.29, bf16[2,4,2,8,16,128]{5,4,3,2,1,0:T(8,128)(2,1)S(1)} %bitcast.27, ...), custom_call_target="tpu_custom_call" | custom-call | tf_op jit(solution)/shard_map/pallas_call | solution.py:252
  66.2 0.7 %reshape.28 = f32[2,2,8,2048]{3,2,1,0:T(8,128)} reshape(f32[2,2,8,16,128]{4,3,2,1,0:T(8,128)S(1)} %get-tuple-element.4) | data formatting | bytes 524288 | tf_op jit(solution)/shard_map/reshape | solution.py:286
  67.0 0.7 %reshape.29 = f32[2,2,8,2048]{3,2,1,0:T(8,128)} reshape(f32[2,2,8,16,128]{4,3,2,1,0:T(8,128)S(1)} %get-tuple-element.5) | data formatting | bytes 524288 | tf_op jit(solution)/shard_map/reshape | solution.py:286
  (3 shorter events, 0.1 us)
Async XLA Ops:
  0.6 2.7 %copy-start.1 = (f32[2,2,8,2048]{3,2,1,0:T(8,128)S(1)}, f32[2,2,8,2048]{3,2,1,0:T(8,128)}, u32[]{:S(2)}) copy-start(f32[2,2,8,2048]{3,2,1,0:T(8,128)} %param.6) | copy-start | bytes 786436
  2.4 1.1 %copy-start.2 = (f32[2,2,8,2048]{3,2,1,0:T(8,128)S(1)}, f32[2,2,8,2048]{3,2,1,0:T(8,128)}, u32[]{:S(2)}) copy-start(f32[2,2,8,2048]{3,2,1,0:T(8,128)} %param.7) | copy-start | bytes 786436
  3.4 1.0 %copy-start = (bf16[2,4,2,8,2048]{4,3,2,1,0:T(8,128)(2,1)S(1)}, bf16[2,4,2,8,2048]{4,3,2,1,0:T(8,128)(2,1)}, u32[]{:S(2)}) copy-start(bf16[2,4,2,8,2048]{4,3,2,1,0:T(8,128)(2,1)} %param.8) | copy-start | bytes 1572868

commit v3 on v2

--- a/solution.py
+++ b/solution.py
@@ -114,6 +114,18 @@
         return jnp.where(place > lanes - 1, after, jnp.where(place < 0, before, turned))
 
     ext[:, REACH : REACH + count, UP : UP + height] = u_ref[...]
+    barrier = pltpu.get_barrier_semaphore()
+    mates = [(lax.rem(my_sec + turn, n_sec), my_tile) for turn in range(1, n_sec)]
+    mates += [(my_sec, lax.rem(my_tile + turn, n_tile)) for turn in range(1, n_tile)]
+    for mate in mates:
+        pl.semaphore_signal(barrier, inc=1, device_id=mate, device_id_type=MESH)
+    corners = [(a, b) for a, b in ways if a != 0 and b != 0]
+    for a, b in corners:
+        def greet(a=a, b=b):
+            pl.semaphore_signal(barrier, inc=1, device_id=(my_sec + a, my_tile + b), device_id_type=MESH)
+        pl.when(there(a, b))(greet)
+    met = len(mates) + sum(there(a, b).astype(jnp.int32) for a, b in corners)
+    pl.semaphore_wait(barrier, met)
     send_halo(ext, 0)
     trans_copy = spread(trans_ref, trans_all, tr_send, tr_recv, n_sec, my_sec, along_sec)
     keep[...] = (1 - fixed_ref[...]).astype(jnp.float32)
@@ -274,7 +286,7 @@
             dma((ITERS, n_tile)),
             dma((ITERS, n_tile)),
         ],
-        compiler_params=pltpu.CompilerParams(has_side_effects=True, vmem_limit_bytes=40 * 2**20),
+        compiler_params=pltpu.CompilerParams(collective_id=0, has_side_effects=True, vmem_limit_bytes=40 * 2**20),
     )(
         shift,
         displacement.reshape(cells),

time: 67.9 us -> 64 us (0.943)
  Pallas kernels: 61.7 us -> 57.7 us
    pallas_call x1, Pallas kernels: 61.7 us -> 57.7 us  [shards(): pl.pallas_call(functools.partial(kernel, n_sec, n_tile), out_shape=(jax.S...]
where the time goes in v3:
time: 64 us; the launch traced here: 63.8 us
  Pallas kernels  57.7 us (90%)
  local copies, waits for them, and re-layouts  5.35 us (8%)
  between operations  0.7 us (1%)
    pallas_call x1, Pallas kernels, shards(): pl.pallas_call(functools.partial(kernel, n_sec, n_tile), out_shape=(jax.S...  57.7 us
    unnamed x11, local copies, waits for them, and re-layouts  2.88 us
    reshape x2, local copies, waits for them, and re-layouts, shards(): return (u.reshape(displacement.shape), v.reshape(displacement.shape))  1.5 us

profile of v3, /device:TPU:0, one launch (start us, length us, event | category | flops | bytes accessed | tf_op | source)
XLA Modules:
  0.0 63.8 jit_solution(2253533397938755267)
XLA Ops:
  0.6 0.0 copy-start.1
  0.6 0.8 %broadcast_in_dim.2 = f32[4]{0:T(128)S(1)} reshape(f32[2,2]{1,0:T(2,128)} %param.11) | data formatting | bytes 32 | tf_op jit(solution)/shard_map/broadcast_in_dim | solution.py:259
  1.4 0.1 pad.7.trans_ref
  1.5 0.8 %copy.9 = s32[4,2,1,2]{3,1,0,2:T(2,128)S(1)} copy(s32[4,2,1,2]{0,3,2,1:T(2,128)} %param.9) | data formatting | bytes 128 | tf_op args[3]
  2.3 0.1 reshape_squeeze.3.off_ref
  2.4 0.0 copy-start.2
  2.4 1.0 %copy.15 = s32[2,8,16,128]{3,2,1,0:T(8,128)S(1)} copy(s32[2,8,16,128]{3,1,2,0:T(8,128)} %bitcast.33) | data formatting | bytes 262144
  3.4 0.0 copy-done.1
  3.4 0.0 copy-start
  3.4 0.0 copy-done.2
  3.5 0.9 %copy-done = bf16[2,4,2,8,2048]{4,3,2,1,0:T(8,128)(2,1)S(1)} copy-done((bf16[2,4,2,8,2048]{4,3,2,1,0:T(8,128)(2,1)S(1)}, bf16[2,4,2,8,2048]{4,3,2,1,0:T(8,128)(2,1)}, u32[]{:S(2)}) %copy-start) | copy-done | bytes 524312
  4.4 0.1 copy.12
  4.5 57.7 %shard_map.77 = (f32[2,2,8,16,128]{4,3,2,1,0:T(8,128)S(1)}, f32[2,2,8,16,128]{4,3,2,1,0:T(8,128)S(1)}) custom-call(s32[16]{0:T(128)S(1)} %reshape_squeeze.3.off_ref, f32[2,2,8,16,128]{4,3,2,1,0:T(8,128)S(1)} %bitcast.28, f32[2,2,8,16,128]{4,3,2,1,0:T(8,128)S(1)} %bitcast.29, bf16[2,4,2,8,16,128]{5,4,3,2,1,0:T(8,128)(2,1)S(1)} %bitcast.27, ...), custom_call_target="tpu_custom_call" | custom-call | tf_op jit(solution)/shard_map/pallas_call | solution.py:264
  62.3 0.7 %reshape.28 = f32[2,2,8,2048]{3,2,1,0:T(8,128)} reshape(f32[2,2,8,16,128]{4,3,2,1,0:T(8,128)S(1)} %get-tuple-element.4) | data formatting | bytes 524288 | tf_op jit(solution)/shard_map/reshape | solution.py:298
  63.0 0.7 %reshape.29 = f32[2,2,8,2048]{3,2,1,0:T(8,128)} reshape(f32[2,2,8,16,128]{4,3,2,1,0:T(8,128)S(1)} %get-tuple-element.5) | data formatting | bytes 524288 | tf_op jit(solution)/shard_map/reshape | solution.py:298
  (3 shorter events, 0.1 us)
Async XLA Ops:
  0.6 2.7 %copy-start.1 = (f32[2,2,8,2048]{3,2,1,0:T(8,128)S(1)}, f32[2,2,8,2048]{3,2,1,0:T(8,128)}, u32[]{:S(2)}) copy-start(f32[2,2,8,2048]{3,2,1,0:T(8,128)} %param.6) | copy-start | bytes 786436
  2.4 1.1 %copy-start.2 = (f32[2,2,8,2048]{3,2,1,0:T(8,128)S(1)}, f32[2,2,8,2048]{3,2,1,0:T(8,128)}, u32[]{:S(2)}) copy-start(f32[2,2,8,2048]{3,2,1,0:T(8,128)} %param.7) | copy-start | bytes 786436
  3.4 1.0 %copy-start = (bf16[2,4,2,8,2048]{4,3,2,1,0:T(8,128)(2,1)S(1)}, bf16[2,4,2,8,2048]{4,3,2,1,0:T(8,128)(2,1)}, u32[]{:S(2)}) copy-start(bf16[2,4,2,8,2048]{4,3,2,1,0:T(8,128)(2,1)} %param.8) | copy-start | bytes 1572868
